TPU v7x, 128 devices: a whole 4x4x4 slice. The times are simulated.
128 devices in a mesh: depth: 16 (over x, z_lo, core), group: 8 (over z_hi, y).
Axes of the slice: x: 4, y: 4, z: 4 (z_hi: 2, z_lo: 2; z = z_hi * 2 + z_lo), core: 2. Of those that a mesh axis runs over, the one named last changes fastest.
Arguments:
- output_one: bfloat16 [32, 256, 128, 128], P(None, 'depth', 'group'), may hold values from -6 to 6
- output_two: bfloat16 [32, 256, 128, 128], P(None, 'depth', 'group'), may hold values from -6 to 6
- cotangent_one: bfloat16 [32, 256, 128, 128], P(None, 'depth', 'group'), may hold values from -6 to 6
- cotangent_two: bfloat16 [32, 256, 128, 128], P(None, 'depth', 'group'), may hold values from -6 to 6
- first_weight: bfloat16 [27, 32, 32], replicated, may hold values from -0.21875 to 0.21875
- second_weight: bfloat16 [27, 32, 32], replicated, may hold values from -0.21875 to 0.21875
- bricks: int32 [16, 8, 8], P('depth'), may hold values from 0 to 8, as said below
Outputs:
- restored_one: bfloat16 [32, 256, 128, 128], P(None, 'depth', 'group')
- restored_two: bfloat16 [32, 256, 128, 128], P(None, 'depth', 'group')
- input_grad_one: bfloat16 [32, 256, 128, 128], P(None, 'depth', 'group')
- input_grad_two: bfloat16 [32, 256, 128, 128], P(None, 'depth', 'group')
- first_weight_grad: float32 [27, 32, 32], replicated
- second_weight_grad: float32 [27, 32, 32], replicated
Inputs may be any that keep to these rules, and one draw needn't show every extreme that they name: bricks[z, g, :] lists the positions of the occupied bricks of depth layer z and lateral row g, distinct and ascending, followed by 8 in every unused entry. For each z the numbers of occupied bricks over g = 0 .. 7 are a reordering of 1 + (7 * j * j) // 49 for j = 0 .. 7, so in every depth layer one row has all 8 bricks occupied and the layer holds at most 32 occupied bricks.
All inputs are finite; a program needn't handle non-finite values.
Results may differ from a plain program's by a relative error of at most 0.0085.
Values may be sent and summed in bfloat16 or wider, within the bound.
A program may use at most 256 MiB of HBM per device.

v0:
```python
import math

import jax
import jax.numpy as jnp
from jax import lax
from jax.sharding import PartitionSpec as P


def extended_2(shard, sides, width):
    for axis, dim in sides:
        size, length = (lax.axis_size(axis), shard.shape[dim])
        up = [(i, (i + 1) % size) for i in range(size - 1)]
        down = [(j, i) for i, j in up]
        last = lax.slice_in_dim(shard, length - width, length, axis=dim)
        initial = lax.slice_in_dim(shard, 0, width, axis=dim)
        before = lax.ppermute(last, axis, up)
        after = lax.ppermute(initial, axis, down)
        shard = jnp.concatenate([before, shard, after], axis=dim)
    return shard


def logistic_slope(inputs):
    logistic = jax.nn.sigmoid(inputs)
    return logistic * (1.0 + inputs * (1.0 - logistic))


def tap_offsets(brick_edge):
    window_edge = brick_edge + 2
    offsets = []
    for depth_step in range(3):
        for row_step in range(3):
            for col_step in range(3):
                offsets.append(
                    depth_step * window_edge * window_edge + row_step * window_edge + col_step
                )
    return offsets


def grid_length(brick_edge):
    window_edge = brick_edge + 2
    return (
        (brick_edge - 1) * window_edge * window_edge + (brick_edge - 1) * window_edge + brick_edge
    )


def padded_length(brick_edge):
    return (grid_length(brick_edge) + 127) // 128 * 128


def extend(window, brick_edge):
    needed = max(tap_offsets(brick_edge)) + padded_length(brick_edge)
    return jnp.pad(window, ((0, 0), (0, max(needed - window.shape[1], 0))))


def convolve(window, kernel, brick_edge):
    length = padded_length(brick_edge)
    total = jnp.zeros((kernel.shape[1], length), jnp.float32)
    for number, offset in enumerate(tap_offsets(brick_edge)):
        total = total + jnp.dot(
            kernel[number], window[:, offset : offset + length], preferred_element_type=jnp.float32
        )
    return total


def grid_to_brick(values, brick_edge):
    window_edge = brick_edge + 2
    channels = values.shape[0]
    full_size = brick_edge * window_edge * window_edge
    values = values[:, : grid_length(brick_edge)]
    padded = jnp.pad(values, ((0, 0), (0, full_size - values.shape[1])))
    cubes = padded.reshape(channels, brick_edge, window_edge, window_edge)[
        :, :, :brick_edge, :brick_edge
    ]
    return cubes.reshape(channels, brick_edge**3)


def brick_to_grid(values, brick_edge):
    channels = values.shape[0]
    cubes = values.reshape(channels, brick_edge, brick_edge, brick_edge)
    padded = jnp.pad(cubes, ((0, 0), (0, 0), (0, 2), (0, 2)))
    grid = padded.reshape(channels, -1)[:, : grid_length(brick_edge)]
    return jnp.pad(grid, ((0, 0), (0, padded_length(brick_edge) - grid_length(brick_edge))))


def centre(window, brick_edge):
    window_edge = brick_edge + 2
    offset = window_edge * window_edge + window_edge + 1
    return grid_to_brick(window[:, offset : offset + grid_length(brick_edge)], brick_edge)


def weight_gradient(errors, window, brick_edge):
    grid = brick_to_grid(errors, brick_edge)
    length = padded_length(brick_edge)
    pieces = []
    for offset in tap_offsets(brick_edge):
        pieces.append(
            lax.dot_general(
                grid,
                window[:, offset : offset + length],
                (((1,), (1,)), ((), ())),
                preferred_element_type=jnp.float32,
            )
        )
    return jnp.stack(pieces, axis=0)


def first_round(windows, kernels, brick_edge):
    source = extend(windows[0], brick_edge)
    preact = grid_to_brick(convolve(source, kernels[1], brick_edge), brick_edge)
    cotangent = centre(windows[1], brick_edge).astype(jnp.float32)
    shaped = jax.nn.silu(preact).astype(jnp.bfloat16)
    errors = (cotangent * logistic_slope(preact)).astype(jnp.bfloat16)
    return (jnp.stack([shaped, errors]), weight_gradient(errors, source, brick_edge))


def second_round(windows, kernels, brick_edge):
    source = extend(windows[0], brick_edge)
    preact = grid_to_brick(convolve(source, kernels[0], brick_edge), brick_edge)
    spread = grid_to_brick(
        convolve(extend(windows[1], brick_edge), kernels[3], brick_edge), brick_edge
    )
    totals = (centre(windows[2], brick_edge).astype(jnp.float32) + spread).astype(jnp.bfloat16)
    shaped = jax.nn.silu(preact).astype(jnp.bfloat16)
    errors = (totals.astype(jnp.float32) * logistic_slope(preact)).astype(jnp.bfloat16)
    return (jnp.stack([totals, shaped, errors]), weight_gradient(errors, source, brick_edge))


def third_round(windows, kernels, brick_edge):
    spread = grid_to_brick(
        convolve(extend(windows[0], brick_edge), kernels[2], brick_edge), brick_edge
    )
    result = (centre(windows[1], brick_edge).astype(jnp.float32) + spread).astype(jnp.bfloat16)
    channels = result.shape[0]
    return (result[None], jnp.zeros((27, channels, channels), jnp.float32))


def cut_window(padded, offset, brick_edge):
    window_edge = brick_edge + 2
    anchor = jnp.zeros((), jnp.int32)
    block = lax.dynamic_slice(
        padded,
        (anchor, anchor, anchor, anchor, offset),
        (padded.shape[0], padded.shape[1], window_edge, window_edge, window_edge),
    )
    return block.reshape(padded.shape[0], padded.shape[1], window_edge**3)


def with_faces(stacked):
    extended = extended_2(stacked, (("depth", 2), ("group", 3)), 1)
    return jnp.pad(extended, ((0, 0), (0, 0), (0, 0), (0, 0), (1, 1)))


def zero_rim(volume):
    return jnp.pad(volume[None], ((0, 0), (0, 0), (1, 1), (1, 1), (1, 1)))


def own_pass(padded, initial, compute, own_list, own_count, brick_edge, grad_shape):

    def visit(number, state):
        slab_stack, partials = state
        offset = own_list[number] * brick_edge
        bricks_out, gradient = compute(cut_window(padded, offset, brick_edge))
        cubes = bricks_out.reshape(
            bricks_out.shape[0], bricks_out.shape[1], brick_edge, brick_edge, brick_edge
        )
        anchor = jnp.zeros((), jnp.int32)
        slab_stack = lax.dynamic_update_slice(
            slab_stack, cubes, (anchor, anchor, anchor, anchor, offset)
        )
        return (slab_stack, partials + gradient)

    return lax.fori_loop(0, own_count, visit, (initial, jnp.zeros(grad_shape, jnp.float32)))


def local(
    output_one, output_two, cotangent_one, cotangent_two, first_weight, second_weight, bricks
):
    brick_edge = output_one.shape[1]
    across = output_one.shape[3]
    slots = bricks.shape[2]
    groups = lax.axis_size("group")
    position = lax.axis_index("group")
    listing = bricks[0]
    counts = jnp.sum((listing < slots).astype(jnp.int32), axis=1)
    own_list = listing[position]
    own_count = counts[position]
    present = jnp.any(own_list[:, None] == jnp.arange(slots, dtype=jnp.int32)[None, :], axis=0)
    column_mask = jnp.repeat(present.astype(jnp.float32), brick_edge)
    kernels = (
        first_weight,
        second_weight,
        jnp.transpose(jnp.flip(first_weight, 0), (0, 2, 1)),
        jnp.transpose(jnp.flip(second_weight, 0), (0, 2, 1)),
    )
    grad_shape = first_weight.shape

    def run_round(padded, initial, compute):
        return own_pass(padded, initial, compute, own_list, own_count, brick_edge, grad_shape)

    zeros_volume = jnp.zeros_like(output_one)
    upper_masked = (output_one.astype(jnp.float32) * column_mask).astype(jnp.bfloat16)
    padded = jnp.concatenate([with_faces(upper_masked[None]), zero_rim(cotangent_two)], axis=0)
    first_stack, second_partial = run_round(
        padded,
        jnp.stack([zeros_volume, zeros_volume]),
        lambda windows: first_round(windows, kernels, brick_edge),
    )
    restored_two = (output_two.astype(jnp.float32) - first_stack[0].astype(jnp.float32)).astype(
        jnp.bfloat16
    )
    lower_masked = (restored_two.astype(jnp.float32) * column_mask).astype(jnp.bfloat16)
    padded = jnp.concatenate(
        [with_faces(jnp.stack([lower_masked, first_stack[1]])), zero_rim(cotangent_one)], axis=0
    )
    second_stack, first_partial = run_round(
        padded,
        jnp.stack([cotangent_one, zeros_volume, zeros_volume]),
        lambda windows: second_round(windows, kernels, brick_edge),
    )
    input_grad_one = second_stack[0]
    restored_one = (output_one.astype(jnp.float32) - second_stack[1].astype(jnp.float32)).astype(
        jnp.bfloat16
    )
    padded = jnp.concatenate([with_faces(second_stack[2][None]), zero_rim(cotangent_two)], axis=0)
    third_stack, unused = run_round(
        padded, cotangent_two[None], lambda windows: third_round(windows, kernels, brick_edge)
    )
    input_grad_two = third_stack[0]
    first_total, second_total = lax.psum((first_partial, second_partial), ("depth", "group"))
    scale = 1.0 / math.sqrt(
        float(brick_edge * lax.axis_size("depth") * brick_edge * groups * across)
    )
    return (
        restored_one,
        restored_two,
        input_grad_one,
        input_grad_two,
        first_total * scale,
        second_total * scale,
    )


def solution(mesh):
    placed = (
        P(None, "depth", "group", None),
        P(None, "depth", "group", None),
        P(None, "depth", "group", None),
        P(None, "depth", "group", None),
        P(),
        P(),
        P("depth", None, None),
    )
    return jax.shard_map(
        local,
        mesh=mesh,
        in_specs=placed,
        out_specs=(
            P(None, "depth", "group", None),
            P(None, "depth", "group", None),
            P(None, "depth", "group", None),
            P(None, "depth", "group", None),
            P(),
            P(),
        ),
        check_vma=False,
    )
```

profile of v0, /device:TPU:19, one launch (start us, length us, event | category | flops | bytes accessed | tf_op | source)
XLA Modules:
  0.0 2377.2 jit_solution(3868403022344537822)
XLA Ops:
  33.8 6.9 select_maximum_fusion.6
  40.8 9.6 fusion.928
  50.4 22.5 copy.67
  72.8 6.4 broadcast.173
  80.0 612.9 %while.40 = (s32[]{:T(128)}, bf16[2,32,16,16,128]{1,4,3,2,0:T(8,128)(2,1)}, f32[27,32,32]{2,1,0:T(8,128)}, s32[]{:T(128)}, s32[8]{0:T(128)S(1)}, /*index=5*/bf16...) while((s32[]{:T(128)}, ...), condition=%wide.region_3.4_spmd, body=%wide.region_2.3_spmd.sunk | while | flops 587555840 | bytes 164357712 | solution.py:172
  105.2 6.3 constant_dynamic-slice_fusion.10
  178.0 6.3 constant_dynamic-slice_fusion.10
  250.8 6.3 constant_dynamic-slice_fusion.10
  323.5 6.3 constant_dynamic-slice_fusion.10
  469.0 6.3 constant_dynamic-slice_fusion.10
  692.9 15.1 copy.68
  744.8 17.1 stack.360.clone
  768.3 14.0 select_maximum_fusion
  782.3 6.8 fusion.920
  789.1 33.0 %copy.72 = bf16[3,32,18,18,130]{1,4,3,2,0:T(8,128)(2,1)} copy(bf16[3,32,18,18,130]{4,1,3,2,0:T(8,128)(2,1)} %fusion.920) | data formatting | bytes 16174080 | tf_op jit(solution)/shard_map/while | solution.py:172
  823.0 965.3 %while.41 = (s32[]{:T(128)}, bf16[3,32,16,16,128]{1,4,3,2,0:T(8,128)(2,1)}, f32[27,32,32]{2,1,0:T(8,128)}, s32[]{:T(128)}, s32[8]{0:T(128)S(1)}, /*index=5*/bf16...) while((s32[]{:T(128)}, ...), condition=%wide.region_5.6_spmd, body=%wide.region_4.5_spmd.sunk | while | flops 883973120 | bytes 240212160 | solution.py:172
  825.1 8.9 constant_dynamic-slice_fusion.11
  945.0 8.9 constant_dynamic-slice_fusion.11
  1064.5 9.0 constant_dynamic-slice_fusion.11
  1184.3 9.0 constant_dynamic-slice_fusion.11
  1303.8 8.9 constant_dynamic-slice_fusion.11
  1423.4 8.9 constant_dynamic-slice_fusion.11
  1543.0 8.9 constant_dynamic-slice_fusion.11
  1662.7 8.3 constant_dynamic-slice_fusion.11
  1788.3 22.0 copy.73
  1815.7 23.4 copy.74
  1856.7 145.0 %all-reduce.20.cloned.1.call-done = (f32[27,32,32]{2,1,0:T(8,128)}, f32[27,32,32]{2,1,0:T(8,128)}) async-done(((f32[27,32,32]{2,1,0:T(8,128)}, f32[27,32,32]{2,1,0:T(8,128)}), (f32[27,32,32]{2,1,0:T(8,128)}, f32[27,32,32]{2,1,0:T(8,128)})) %all-reduce.20.cloned.1.call-update) | async-done | bytes 221200 | tf_op jit(solution)/shard_map/psum | solution.py:229
  2003.8 8.2 select_maximum_fusion.2
  2012.0 9.6 fusion.929
  2021.6 22.5 copy.80
  2044.1 317.2 %while.42 = (s32[]{:T(128)}, bf16[1,32,16,16,128]{1,4,3,2,0:T(8,128)(2,1)}, s32[]{:T(128)}, s32[8]{0:T(128)S(1)}, bf16[2,32,18,18,130]{1,4,3,2,0:T(8,128)(2,1)},...) while((s32[]{:T(128)}, ...), condition=%wide.region_7.8_spmd, body=%wide.region_6.7_spmd.sunk | while | flops 295106560 | bytes 87847184 | solution.py:172
  2361.4 8.6 copy.81
  (1937 shorter events, 1805.9 us)
Async XLA Ops:
  7.2 1994.5 %all-reduce.20.cloned.1.call-start = ((), (), s32[]{:S(2)}) async-start(), calls=%async_computation | async-start | bytes 1769472 | tf_op jit(solution)/shard_map/psum | solution.py:229
  11.1 10.5 copy-start.16
  11.2 6.0 collective-permute-start
  15.3 6.3 collective-permute-start.1
  21.6 9.4 collective-permute-start.2
  24.5 9.3 collective-permute-start.3
  26.9 6.9 copy-start.17
  30.1 10.7 copy-start.5
  692.9 17.2 copy-start.26
  692.9 17.2 copy-start.28
  710.9 12.9 copy-start.8
  713.9 9.8 copy-start.10
  714.0 5.2 collective-permute-start.4
  715.9 13.9 copy-start.23
  715.9 7.8 collective-permute-start.5
  723.8 6.3 copy-start.6
  724.6 43.7 %collective-permute-start.6 = (bf16[2,32,18,1,128]{4,1,3,2,0:T(8,128)(2,1)}, bf16[2,32,18,1,128]{4,1,3,2,0:T(8,128)(2,1)}, u32[]{:S(2)}, u32[]{:S(2)}) collective-permute-start(bf16[2,32,18,1,128]{4,1,3,2,0:T(8,128)(2,1)} %get-tuple-element.429), channel_id=1, source_target_pairs={{0,1},{1,2},{2,3},{3,4},{4,5},{5,6},{6,7},{8,9},{9,10},{10,11},{11... | collective-permute-start | bytes 884744 | tf_op jit(solution)/shard_map/ppermute | solution.py:16
  726.5 41.8 %collective-permute-start.7 = (bf16[2,32,18,1,128]{4,1,3,2,0:T(8,128)(2,1)S(1)}, bf16[2,32,18,1,128]{4,1,3,2,0:T(8,128)(2,1)}, u32[]{:S(2)}, u32[]{:S(2)}) collective-permute-start(bf16[2,32,18,1,128]{4,1,3,2,0:T(8,128)(2,1)S(1)} %get-tuple-element.430), channel_id=1, source_target_pairs={{1,0},{2,1},{3,2},{4,3},{5,4},{6,5},{7,6},{9,8},{10,9},{11,10},{12... | collective-permute-start | bytes 884744 | tf_op jit(solution)/shard_map/ppermute | solution.py:17
  1788.3 23.0 copy-start.20
  1839.1 12.2 collective-permute-start.8
  1841.4 9.9 collective-permute-start.9
  1851.4 152.4 %collective-permute-start.10 = (bf16[1,32,18,1,128]{4,1,3,2,0:T(8,128)(2,1)S(1)}, bf16[1,32,18,1,128]{4,1,3,2,0:T(8,128)(2,1)S(1)}, u32[]{:S(2)}, u32[]{:S(2)}) collective-permute-start(bf16[1,32,18,1,128]{4,1,3,2,0:T(8,128)(2,1)S(1)} %get-tuple-element.433), channel_id=1, source_target_pairs={{0,1},{1,2},{2,3},{3,4},{4,5},{5,6},{6,7},{8,9},{9,10},{10,11},{11... | collective-permute-start | bytes 442376 | tf_op jit(solution)/shard_map/ppermute | solution.py:16
  1853.3 150.5 %collective-permute-start.11 = (bf16[1,32,18,1,128]{4,1,3,2,0:T(8,128)(2,1)S(1)}, bf16[1,32,18,1,128]{4,1,3,2,0:T(8,128)(2,1)S(1)}, u32[]{:S(2)}, u32[]{:S(2)}) collective-permute-start(bf16[1,32,18,1,128]{4,1,3,2,0:T(8,128)(2,1)S(1)} %get-tuple-element.434), channel_id=1, source_target_pairs={{1,0},{2,1},{3,2},{4,3},{5,4},{6,5},{7,6},{9,8},{10,9},{11,10},{12... | collective-permute-start | bytes 442376 | tf_op jit(solution)/shard_map/ppermute | solution.py:17
  2003.8 8.2 copy-start.7
  2076.3 5.1 copy-start
  2115.9 5.1 copy-start
  2155.4 5.1 copy-start
  2195.0 5.1 copy-start
  2234.5 5.1 copy-start
  2274.1 5.1 copy-start
  2313.6 5.1 copy-start
  2352.8 5.1 copy-start
  (95 other events, 208.8 us)
Sparse Core Ops, SparseCore 0:
  1851.4 150.1 all-reduce.19
where the time goes:
time: 2410 us; the launch traced here: 2380 us
  matrix products  934 us (39%)
  local copies, waits for them, and re-layouts  918 us (38%)
  other arithmetic  239 us (10%)
  waiting for transfers between devices  157 us (7%)
  loops' own time  83.2 us (3%)
  starting transfers between devices  30.7 us (1%)
    dot_general x864, matrix products, convolve(): jnp.dot(kernel[number], window[:, offset:offset + length], preferred_elem...  639 us
    dot_general x432, matrix products, weight_gradient(): lax.dot_general(grid, window[:, offset:offset + length], (((1,), (1,)), (...  296 us
    reshape x56, local copies, waits for them, and re-layouts, grid_to_brick(): padded.reshape(channels, brick_edge, window_edge, window_edge)  169 us
    while x8, local copies, waits for them, and re-layouts, own_pass(): lax.fori_loop(0, own_count, visit, (initial, jnp.zeros(grad_shape, jnp.fl...  153 us
    psum x1, waiting for transfers between devices, local(): lax.psum((first_partial, second_partial), ('depth', 'group'))  145 us
    pad x56, local copies, waits for them, and re-layouts, grid_to_brick(): padded = jnp.pad(values, ((0, 0), (0, full_size - values.shape[1])))  84.9 us
    another operation x3, loops' own time, own_pass(): lax.fori_loop(0, own_count, visit, (initial, jnp.zeros(grad_shape, jnp.fl...  83.2 us
    slice x8, local copies, waits for them, and re-layouts, second_round(): windows[2]  71 us
  transfers between devices with their start and end apart: 13, of which 5 were waited for; matrix products, arithmetic and copies ran while one was open for 2% of the time, Pallas kernels for 0%

commit v1 on v0

v1 whole, which is shorter than its diff:
```python
import math

import jax
import jax.numpy as jnp
from jax import lax
from jax.experimental import pallas as pl
from jax.experimental.pallas import tpu as pltpu
from jax.sharding import PartitionSpec as P

MESH = pl.DeviceIdType.MESH
BF = jnp.bfloat16
F32 = jnp.float32

CH = 32
B = 16
NX = 128
ND = 16
NG = 8
CHUNKS = 12
DIRS = tuple((dz, dy) for dz in (-1, 0, 1) for dy in (-1, 0, 1) if (dz, dy) != (0, 0))


def dot(a, b):
    return lax.dot_general(a, b, (((1,), (0,)), ((), ())), preferred_element_type=F32)


def dot_nt(a, b):
    return lax.dot_general(a, b, (((1,), (1,)), ((), ())), preferred_element_type=F32)


def permutation():
    row = lax.broadcasted_iota(jnp.int32, (256, 256), 0)
    col = lax.broadcasted_iota(jnp.int32, (256, 256), 1)
    return jnp.where((row & 15) * 16 + (row >> 4) == col, 1.0, 0.0).astype(BF)


def lane():
    return lax.broadcasted_iota(jnp.int32, (1, NX), 1)


def shift_up(values):
    return jnp.where(lane() == 0, 0.0, pltpu.roll(values, 1, 1))


def shift_down(values):
    return jnp.where(lane() == NX - 1, 0.0, pltpu.roll(values, NX - 1, 1))


def band_rows(blocks, out_ref):
    zeros = jnp.zeros((CH, NX), F32)
    for c in range(3):
        wide = jnp.concatenate([blocks(a, c) for a in range(3)] + [zeros], axis=1)
        for zo in range(2):
            for yo in range(2):
                turn = (zo * 4 + yo) * CH
                moved = wide if turn == 0 else pltpu.roll(wide, turn, 1)
                row = (c * 4 + zo * 2 + yo) * CH
                out_ref[row : row + CH, :] = moved.astype(BF)


def build_band(w_ref, out_ref):
    def blocks(a, c):
        taps = [w_ref[9 * a + 3 * b + c].astype(F32) for b in range(3)]
        return jnp.concatenate(taps + [jnp.zeros((CH, CH), F32)], axis=1)

    band_rows(blocks, out_ref)


def build_band_transposed(w_ref, out_ref):
    def blocks(a, c):
        taps = [w_ref[26 - (9 * a + 3 * b + c)].astype(F32) for b in range(3)]
        tall = jnp.concatenate(taps + [jnp.zeros((CH, CH), F32)], axis=0)
        square = jnp.concatenate([tall, jnp.zeros((NX, NX - CH), F32)], axis=1)
        return jnp.transpose(square)[:CH]

    band_rows(blocks, out_ref)


def fused(
    o1, o2, c1, c2, w1_ref, w2_ref, bricks_ref,
    r1_out, r2_out, g1_out, g2_out, t1_out, t2_out,
    n_o1, n_o2, n_c1, n_c2,
    q_o1, q_o2, q_c1, q_c2,
    p_u, p_l, p_eg, p_ef,
    shifted, perm, band_f, band_g, band_tf, band_tg, acc,
    part, rs_in, ar_in, tot,
    in_sem, out_sem, hs, hr, rs_s, rs_r, ar_s, ar_r, ag_s, ag_r,
):
    depth = lax.axis_index("depth")
    group = lax.axis_index("group")

    def exists(dz, dy):
        ok = None
        for d, at, size in ((dz, depth, ND), (dy, group, NG)):
            if d == 0:
                continue
            here = at > 0 if d < 0 else at < size - 1
            ok = here if ok is None else jnp.logical_and(ok, here)
        return ok

    def clamp(dz, dy):
        return (
            jnp.clip(depth + dz, 0, ND - 1) if dz else depth,
            jnp.clip(group + dy, 0, NG - 1) if dy else group,
        )

    loads = [
        pltpu.make_async_copy(src, dst, in_sem.at[n])
        for n, (src, dst) in enumerate(((o1, n_o1), (c2, n_c2), (o2, n_o2), (c1, n_c1)))
    ]
    for load in loads:
        load.start()

    barrier = pltpu.get_barrier_semaphore()

    def greet_depth(k, _):
        pl.semaphore_signal(
            barrier, inc=1, device_id=(lax.rem(depth + k, ND), group), device_id_type=MESH
        )
        return 0

    def greet_group(k, _):
        pl.semaphore_signal(
            barrier, inc=1, device_id=(depth, lax.rem(group + k, NG)), device_id_type=MESH
        )
        return 0

    lax.fori_loop(1, ND, greet_depth, 0)
    lax.fori_loop(1, NG, greet_group, 0)
    for dz, dy in DIRS:
        if dz != 0 and dy != 0:

            @pl.when(exists(dz, dy))
            def _():
                pl.semaphore_signal(barrier, inc=1, device_id=clamp(dz, dy), device_id_type=MESH)

    perm[...] = permutation()
    place = lane() >> 4
    mask = jnp.zeros((1, NX), F32)
    for slot in range(8):
        mask = jnp.where(place == bricks_ref[0, group, slot], 1.0, mask)

    volumes = (p_u, p_l, p_eg, p_ef)

    def zero_plane(ref, z):
        def body(y, _):
            ref[z, y] = jnp.zeros((CH, NX), BF)
            return 0

        lax.fori_loop(0, B + 2, body, 0)

    def zero_row(ref, y):
        def body(z, _):
            ref[z, y] = jnp.zeros((CH, NX), BF)
            return 0

        lax.fori_loop(0, B + 2, body, 0)

    for d, at in ((depth == 0, 0), (depth == ND - 1, B + 1)):

        @pl.when(d)
        def _():
            for ref in volumes:
                zero_plane(ref, at)

    for d, at in ((group == 0, 0), (group == NG - 1, B + 1)):

        @pl.when(d)
        def _():
            for ref in volumes:
                zero_row(ref, at)

    def relayout(src, dst, masked=None):
        def body(k, _):
            for h in range(2):
                pair = jnp.concatenate(
                    [src[pl.ds(16 * h, 16), 2 * k + zz].reshape(256, NX) for zz in range(2)], axis=1
                )
                turned = dot(perm[...], pair)
                for zz in range(2):
                    half = turned[:, NX * zz : NX * (zz + 1)]
                    dst[2 * k + zz, :, 16 * h : 16 * h + 16, :] = half.astype(BF).reshape(16, 16, NX)
                    if masked is not None:
                        masked[2 * k + 1 + zz, 1 : B + 1, 16 * h : 16 * h + 16, :] = (
                            (half * mask).astype(BF).reshape(16, 16, NX)
                        )
            return 0

        lax.fori_loop(0, 8, body, 0)

    def side(d, sending):
        if d == 0:
            return pl.ds(1, B)
        if sending:
            return pl.ds(B if d > 0 else 1, 1)
        return pl.ds(0 if d > 0 else B + 1, 1)

    def halo(number, k):
        dz, dy = DIRS[k]
        ref = volumes[number]
        return pltpu.make_async_remote_copy(
            src_ref=ref.at[side(dz, True), side(dy, True)],
            dst_ref=ref.at[side(dz, False), side(dy, False)],
            send_sem=hs.at[number, k],
            recv_sem=hr.at[number, k],
            device_id=clamp(dz, dy),
            device_id_type=MESH,
        )

    def halo_start(number):
        for k, (dz, dy) in enumerate(DIRS):

            @pl.when(exists(dz, dy))
            def _():
                halo(number, k).start()

    def halo_arrived(number):
        for k, (dz, dy) in enumerate(DIRS):

            @pl.when(exists(-dz, -dy))
            def _():
                halo(number, k).wait_recv()

    def halo_sent(number):
        for k, (dz, dy) in enumerate(DIRS):

            @pl.when(exists(dz, dy))
            def _():
                halo(number, k).wait_send()

    def windows(ref, i, q):
        return jnp.concatenate(
            [ref[pl.ds(2 * i, 4), pl.ds(4 * q + 2 * r, 4)].reshape(512, NX) for r in range(2)],
            axis=1,
        )

    def join(product, r):
        cut = product[:, NX * r : NX * (r + 1)]
        return cut[128:256] + shift_up(cut[0:128]) + shift_down(cut[256:384])

    def get(ref, i, j):
        return ref[pl.ds(2 * i, 2), pl.ds(2 * j, 2)].reshape(128, NX).astype(F32)

    def put(ref, i, j, values):
        ref[pl.ds(2 * i, 2), pl.ds(2 * j, 2)] = values.reshape(2, 2, CH, NX)

    def put_inner(ref, i, j, values):
        ref[pl.ds(2 * i + 1, 2), pl.ds(2 * j + 1, 2)] = values.reshape(2, 2, CH, NX)

    def put_shifted(i, j, errors):
        wide = errors.astype(F32)
        for number, moved in enumerate((shift_down(wide), shift_up(wide))):
            shifted[number, pl.ds(2 * i, 2), pl.ds(2 * j, 2)] = moved.astype(BF).reshape(2, 2, CH, NX)

    def over_patches(body):
        def step(n, _):
            body(lax.div(n, 4), lax.rem(n, 4))
            return 0

        lax.fori_loop(0, 32, step, 0)

    def sigmoid(v):
        return 0.5 + 0.5 * jnp.tanh(0.5 * v)

    def weight_gradient(w, errors_ref, source_ref):
        acc[...] = jnp.zeros_like(acc)

        def body(i, _):
            left, right = [], []
            for j in range(8):
                low = shifted[0, pl.ds(2 * i, 2), 2 * j : 2 * j + 2].reshape(128, NX)
                mid = errors_ref[pl.ds(2 * i + 1, 2), 2 * j + 1 : 2 * j + 3].reshape(128, NX)
                top = shifted[1, pl.ds(2 * i, 2), 2 * j : 2 * j + 2].reshape(128, NX)
                left.append(jnp.concatenate([low, mid, top], axis=0))
                right.append(source_ref[pl.ds(2 * i, 4), 2 * j : 2 * j + 4].reshape(512, NX))
            acc[...] += dot_nt(jnp.concatenate(left, axis=1), jnp.concatenate(right, axis=1))
            return 0

        lax.fori_loop(0, 8, body, 0)
        for c in range(3):
            total = None
            for zo in range(2):
                for yo in range(2):
                    row = (c * 4 + zo * 2 + yo) * CH
                    turn = (zo * 4 + yo) * CH
                    rows = acc[row : row + CH, :]
                    if turn:
                        rows = pltpu.roll(rows, 512 - turn, 1)
                    total = rows if total is None else total + rows
            part[w, 4 * c : 4 * c + 4] = total[:, :384].reshape(4, 8, 384)

    def rs_copy(w, k):
        peer = lax.rem(depth + k, ND)
        return pltpu.make_async_remote_copy(
            src_ref=part.at[w, lax.rem(peer, CHUNKS)],
            dst_ref=rs_in.at[w, depth],
            send_sem=rs_s.at[w, k],
            recv_sem=rs_r.at[w, depth],
            device_id=(peer, group),
            device_id_type=MESH,
        )

    def rs_arrival(w, k):
        peer = lax.rem(depth + k, ND)
        return pltpu.make_async_remote_copy(
            src_ref=part.at[w, 0],
            dst_ref=rs_in.at[w, peer],
            send_sem=rs_s.at[w, k],
            recv_sem=rs_r.at[w, peer],
            device_id=(peer, group),
            device_id_type=MESH,
        )

    def ar_copy(w, k):
        peer = lax.rem(group + k, NG)
        return pltpu.make_async_remote_copy(
            src_ref=ar_in.at[w, group],
            dst_ref=ar_in.at[w, group],
            send_sem=ar_s.at[w, k],
            recv_sem=ar_r.at[w, group],
            device_id=(depth, peer),
            device_id_type=MESH,
        )

    def ar_arrival(w, k):
        peer = lax.rem(group + k, NG)
        return pltpu.make_async_remote_copy(
            src_ref=ar_in.at[w, group],
            dst_ref=ar_in.at[w, peer],
            send_sem=ar_s.at[w, k],
            recv_sem=ar_r.at[w, peer],
            device_id=(depth, peer),
            device_id_type=MESH,
        )

    def ag_copy(w, k):
        peer = lax.rem(depth + k, ND)
        return pltpu.make_async_remote_copy(
            src_ref=tot.at[w, lax.rem(depth, CHUNKS)],
            dst_ref=tot.at[w, lax.rem(depth, CHUNKS)],
            send_sem=ag_s.at[w, k],
            recv_sem=ag_r.at[w, lax.rem(depth, CHUNKS)],
            device_id=(peer, group),
            device_id_type=MESH,
        )

    def ag_arrival(w, k):
        peer = lax.rem(depth + k, ND)
        at = lax.rem(peer, CHUNKS)
        return pltpu.make_async_remote_copy(
            src_ref=tot.at[w, at],
            dst_ref=tot.at[w, at],
            send_sem=ag_s.at[w, k],
            recv_sem=ag_r.at[w, at],
            device_id=(peer, group),
            device_id_type=MESH,
        )

    owner = depth < CHUNKS

    def each_peer(size, act, only_owners=False):
        def body(k, _):
            if only_owners:

                @pl.when(lax.rem(depth + k, ND) < CHUNKS)
                def _():
                    act(k)
            else:
                act(k)
            return 0

        lax.fori_loop(1, size, body, 0)

    def reduce_start(w):
        each_peer(ND, lambda k: rs_copy(w, k).start(), True)

    def reduce_middle(w):
        @pl.when(owner)
        def _():
            rs_in[w, depth] = part[w, lax.rem(depth, CHUNKS)]
            each_peer(ND, lambda k: rs_arrival(w, k).wait_recv())
            ar_in[w, group] = jnp.sum(rs_in[w], axis=0)
            each_peer(NG, lambda k: ar_copy(w, k).start())

    def reduce_spread(w):
        @pl.when(owner)
        def _():
            each_peer(NG, lambda k: ar_arrival(w, k).wait_recv())
            tot[w, lax.rem(depth, CHUNKS)] = jnp.sum(ar_in[w], axis=0)
            each_peer(ND, lambda k: ag_copy(w, k).start())

    def reduce_end(w):
        each_peer(ND, lambda k: ag_arrival(w, k).wait_recv(), True)
        each_peer(ND, lambda k: rs_copy(w, k).wait_send(), True)

        @pl.when(owner)
        def _():
            each_peer(NG, lambda k: ar_copy(w, k).wait_send())
            each_peer(ND, lambda k: ag_copy(w, k).wait_send())

    build_band(w2_ref, band_g)
    loads[0].wait()
    relayout(n_o1, q_o1, p_u)
    near = jnp.minimum(depth, 1) + jnp.minimum(ND - 1 - depth, 1)
    aside = jnp.minimum(group, 1) + jnp.minimum(NG - 1 - group, 1)
    pl.semaphore_wait(barrier, ND - 1 + NG - 1 + near * aside)
    halo_start(0)
    loads[1].wait()
    relayout(n_c2, q_c2)
    loads[2].wait()
    relayout(n_o2, q_o2)
    loads[3].wait()
    relayout(n_c1, q_c1)
    build_band(w1_ref, band_f)
    build_band_transposed(w1_ref, band_tf)
    build_band_transposed(w2_ref, band_tg)
    halo_arrived(0)

    def first(i, q):
        product = dot(band_g[...], windows(p_u, i, q))
        for r in range(2):
            j = 2 * q + r
            v = join(product, r)
            s = sigmoid(v)
            silu = v * s
            shaped = (mask * silu).astype(BF).astype(F32)
            slope = s + silu * (1.0 - s)
            errors = (mask * get(q_c2, i, j) * slope).astype(BF)
            restored = (get(q_o2, i, j) - shaped).astype(BF)
            put(q_o2, i, j, restored)
            put_inner(p_l, i, j, (restored.astype(F32) * mask).astype(BF))
            put_inner(p_eg, i, j, errors)
            put_shifted(i, j, errors)

    over_patches(first)
    halo_start(1)
    halo_start(2)
    out_two = pltpu.make_async_copy(q_o2, r2_out, out_sem.at[0])
    out_two.start()
    weight_gradient(0, p_eg, p_u)
    reduce_start(0)
    halo_arrived(1)
    halo_arrived(2)

    def second(i, q):
        spread = dot(band_tg[...], windows(p_eg, i, q))
        product = dot(band_f[...], windows(p_l, i, q))
        for r in range(2):
            j = 2 * q + r
            total = (get(q_c1, i, j) + mask * join(spread, r)).astype(BF)
            put(q_c1, i, j, total)
            v = join(product, r)
            s = sigmoid(v)
            silu = v * s
            shaped = (mask * silu).astype(BF).astype(F32)
            slope = s + silu * (1.0 - s)
            errors = (mask * total.astype(F32) * slope).astype(BF)
            put(q_o1, i, j, (get(q_o1, i, j) - shaped).astype(BF))
            put_inner(p_ef, i, j, errors)
            put_shifted(i, j, errors)

    over_patches(second)
    halo_start(3)
    out_one = pltpu.make_async_copy(q_o1, r1_out, out_sem.at[1])
    out_one.start()
    out_grad = pltpu.make_async_copy(q_c1, g1_out, out_sem.at[2])
    out_grad.start()
    reduce_middle(0)
    weight_gradient(1, p_ef, p_l)
    reduce_start(1)
    reduce_spread(0)
    halo_arrived(3)

    def third(i, q):
        spread = dot(band_tf[...], windows(p_ef, i, q))
        for r in range(2):
            j = 2 * q + r
            put(q_c2, i, j, (get(q_c2, i, j) + mask * join(spread, r)).astype(BF))

    over_patches(third)
    out_last = pltpu.make_async_copy(q_c2, g2_out, out_sem.at[3])
    out_last.start()
    reduce_middle(1)
    reduce_spread(1)
    reduce_end(0)
    reduce_end(1)
    for number in range(4):
        halo_sent(number)
    t2_out[...] = tot[0]
    t1_out[...] = tot[1]
    for copy in (out_two, out_one, out_grad, out_last):
        copy.wait()


def natural(scale, r1, r2, g1, g2, t1, t2, r1_out, r2_out, g1_out, g2_out, w1_out, w2_out):
    perm = permutation()
    for src, dst in ((r1, r1_out), (r2, r2_out), (g1, g1_out), (g2, g2_out)):
        for h in range(2):
            pair = jnp.concatenate(
                [src[zz, :, 16 * h : 16 * h + 16, :].reshape(256, NX) for zz in range(2)], axis=1
            )
            turned = dot(perm, pair)
            for zz in range(2):
                half = turned[:, NX * zz : NX * (zz + 1)]
                dst[16 * h : 16 * h + 16, zz] = half.astype(BF).reshape(16, 16, NX)

    @pl.when(pl.program_id(0) == 0)
    def _():
        for src, dst in ((t1, w1_out), (t2, w2_out)):
            for c in range(3):
                rows = src[4 * c : 4 * c + 4].reshape(CH, 384) * scale
                for a in range(3):
                    for b in range(3):
                        at = (a * 4 + b) * CH
                        dst[9 * a + 3 * b + c] = rows[:, at : at + CH]


def local(output_one, output_two, cotangent_one, cotangent_two, first_weight, second_weight, bricks):
    turned = jax.ShapeDtypeStruct((B, B, CH, NX), BF)
    sums = jax.ShapeDtypeStruct((CHUNKS, 8, 384), F32)
    hbm = pl.BlockSpec(memory_space=pl.ANY)
    vmem = pl.BlockSpec(memory_space=pltpu.VMEM)
    smem = pl.BlockSpec(memory_space=pltpu.SMEM)
    plain = pltpu.VMEM((CH, B, B, NX), BF)
    flipped = pltpu.VMEM((B, B, CH, NX), BF)
    padded = pltpu.VMEM((B + 2, B + 2, CH, NX), BF)
    band = pltpu.VMEM((384, 512), BF)
    dma = pltpu.SemaphoreType.DMA
    r1, r2, g1, g2, t1, t2 = pl.pallas_call(
        fused,
        out_shape=(turned, turned, turned, turned, sums, sums),
        in_specs=[hbm, hbm, hbm, hbm, vmem, vmem, smem],
        out_specs=(hbm, hbm, hbm, hbm, vmem, vmem),
        scratch_shapes=[plain] * 4
        + [flipped] * 4
        + [padded] * 4
        + [
            pltpu.VMEM((2, B, B, CH, NX), BF),
            pltpu.VMEM((256, 256), BF),
            band,
            band,
            band,
            band,
            pltpu.VMEM((384, 512), F32),
            pltpu.VMEM((2, CHUNKS, 8, 384), F32),
            pltpu.VMEM((2, ND, 8, 384), F32),
            pltpu.VMEM((2, NG, 8, 384), F32),
            pltpu.VMEM((2, CHUNKS, 8, 384), F32),
            dma((4,)),
            dma((4,)),
            dma((4, 8)),
            dma((4, 8)),
            dma((2, ND)),
            dma((2, ND)),
            dma((2, NG)),
            dma((2, NG)),
            dma((2, ND)),
            dma((2, CHUNKS)),
        ],
        compiler_params=pltpu.CompilerParams(
            collective_id=0, has_side_effects=True, vmem_limit_bytes=56 * 1024 * 1024
        ),
        name="fused",
    )(output_one, output_two, cotangent_one, cotangent_two, first_weight, second_weight, bricks)

    scale = 1.0 / math.sqrt(float(B * ND * B * NG * NX))
    block = pl.BlockSpec((2, B, CH, NX), lambda k: (k, 0, 0, 0))
    result = pl.BlockSpec((CH, 2, B, NX), lambda k: (0, k, 0, 0))
    whole = pl.BlockSpec((CHUNKS, 8, 384), lambda k: (0, 0, 0))
    taps = pl.BlockSpec((27, CH, CH), lambda k: (0, 0, 0))
    volume = jax.ShapeDtypeStruct((CH, B, B, NX), BF)
    weight = jax.ShapeDtypeStruct((27, CH, CH), F32)

    def back(*refs):
        natural(scale, *refs)

    return pl.pallas_call(
        back,
        grid=(8,),
        out_shape=(volume, volume, volume, volume, weight, weight),
        in_specs=[block, block, block, block, whole, whole],
        out_specs=(result, result, result, result, taps, taps),
        name="natural",
    )(r1, r2, g1, g2, t1, t2)


def solution(mesh):
    slab = P(None, "depth", "group", None)
    return jax.shard_map(
        local,
        mesh=mesh,
        in_specs=(slab, slab, slab, slab, P(), P(), P("depth", None, None)),
        out_specs=(slab, slab, slab, slab, P(), P()),
        check_vma=False,
    )
```

time: 2410 us -> 110 us (0.05)
  the two profiles are of different devices: /device:TPU:19 before, /device:TPU:1 now
where the time goes in v1:
time: 110 us; the launch traced here: 109 us
  Pallas kernels  109 us (99%)
    pallas_call x1, Pallas kernels, local(): pl.pallas_call(fused, out_shape=(turned, turned, turned, turned, sums, su...  97.6 us
    pallas_call x1, Pallas kernels, local(): pl.pallas_call(back, grid=(8,), out_shape=(volume, volume, volume, volume...  11 us

profile of v1, /device:TPU:1, one launch (start us, length us, event | category | flops | bytes accessed | tf_op | source)
XLA Modules:
  0.0 109.3 jit_solution(15974537968970594098)
XLA Ops:
  0.6 97.6 %fused.1 = (bf16[16,16,32,128]{3,2,1,0:T(8,128)(2,1)}, bf16[16,16,32,128]{3,2,1,0:T(8,128)(2,1)}, bf16[16,16,32,128]{3,2,1,0:T(8,128)(2,1)}, bf16[16,16,32,128]{...) custom-call(bf16[32,16,16,128]{3,2,1,0:T(8,128)(2,1)} %o1.1, bf16[32,16,16,128]{3,2,1,0:T(8,128)(2,1)} %o2.1, ...), custom_call_target="tpu_custom_call" | custom-call | tf_op jit(solution)/shard_map/fused/pallas_call | solution.py:529
  98.3 11.0 %natural.1 = (bf16[32,16,16,128]{3,2,1,0:T(8,128)(2,1)}, bf16[32,16,16,128]{3,2,1,0:T(8,128)(2,1)}, bf16[32,16,16,128]{3,2,1,0:T(8,128)(2,1)}, bf16[32,16,16,128...) custom-call(bf16[16,16,32,128]{3,2,1,0:T(8,128)(2,1)} %get-tuple-element.12.refs_0_, ...), custom_call_target="tpu_custom_call" | custom-call | tf_op jit(solution)/shard_map/natural/pallas_call | solution.py:577

commit v2 on v1

--- a/solution.py
+++ b/solution.py
@@ -186,7 +186,7 @@
                         )
             return 0
 
-        lax.fori_loop(0, 8, body, 0)
+        lax.fori_loop(0, 8, body, 0, unroll=8)
 
     def side(d, sending):
         if d == 0:
@@ -228,10 +228,9 @@
             def _():
                 halo(number, k).wait_send()
 
-    def windows(ref, i, q):
+    def windows(ref, i, pair):
         return jnp.concatenate(
-            [ref[pl.ds(2 * i, 4), pl.ds(4 * q + 2 * r, 4)].reshape(512, NX) for r in range(2)],
-            axis=1,
+            [ref[pl.ds(2 * i, 4), pl.ds(2 * j, 4)].reshape(512, NX) for j in pair], axis=1
         )
 
     def join(product, r):
@@ -252,12 +251,26 @@
         for number, moved in enumerate((shift_down(wide), shift_up(wide))):
             shifted[number, pl.ds(2 * i, 2), pl.ds(2 * j, 2)] = moved.astype(BF).reshape(2, 2, CH, NX)
 
-    def over_patches(body):
-        def step(n, _):
-            body(lax.div(n, 4), lax.rem(n, 4))
-            return 0
-
-        lax.fori_loop(0, 32, step, 0)
+    def inner_patches(body):
+        def step(i, _):
+            for j in (1, 3, 5):
+                body(i, (j, j + 1))
+            return 0
+
+        lax.fori_loop(1, 7, step, 0, unroll=6)
+
+    def outer_patches(body):
+        def sides(i, _):
+            body(i, (0, 7))
+            return 0
+
+        def ends(n, _):
+            j = 2 * lax.rem(n, 4)
+            body(7 * lax.div(n, 4), (j, j + 1))
+            return 0
+
+        lax.fori_loop(1, 7, sides, 0, unroll=6)
+        lax.fori_loop(0, 8, ends, 0, unroll=8)
 
     def sigmoid(v):
         return 0.5 + 0.5 * jnp.tanh(0.5 * v)
@@ -276,7 +289,7 @@
             acc[...] += dot_nt(jnp.concatenate(left, axis=1), jnp.concatenate(right, axis=1))
             return 0
 
-        lax.fori_loop(0, 8, body, 0)
+        lax.fori_loop(0, 8, body, 0, unroll=4)
         for c in range(3):
             total = None
             for zo in range(2):
@@ -414,12 +427,10 @@
     build_band(w1_ref, band_f)
     build_band_transposed(w1_ref, band_tf)
     build_band_transposed(w2_ref, band_tg)
-    halo_arrived(0)
-
-    def first(i, q):
-        product = dot(band_g[...], windows(p_u, i, q))
-        for r in range(2):
-            j = 2 * q + r
+
+    def first(i, pair):
+        product = dot(band_g[...], windows(p_u, i, pair))
+        for r, j in enumerate(pair):
             v = join(product, r)
             s = sigmoid(v)
             silu = v * s
@@ -432,21 +443,20 @@
             put_inner(p_eg, i, j, errors)
             put_shifted(i, j, errors)
 
-    over_patches(first)
+    inner_patches(first)
+    halo_arrived(0)
+    outer_patches(first)
     halo_start(1)
     halo_start(2)
     out_two = pltpu.make_async_copy(q_o2, r2_out, out_sem.at[0])
     out_two.start()
     weight_gradient(0, p_eg, p_u)
     reduce_start(0)
-    halo_arrived(1)
-    halo_arrived(2)
-
-    def second(i, q):
-        spread = dot(band_tg[...], windows(p_eg, i, q))
-        product = dot(band_f[...], windows(p_l, i, q))
-        for r in range(2):
-            j = 2 * q + r
+
+    def second(i, pair):
+        spread = dot(band_tg[...], windows(p_eg, i, pair))
+        product = dot(band_f[...], windows(p_l, i, pair))
+        for r, j in enumerate(pair):
             total = (get(q_c1, i, j) + mask * join(spread, r)).astype(BF)
             put(q_c1, i, j, total)
             v = join(product, r)
@@ -459,7 +469,10 @@
             put_inner(p_ef, i, j, errors)
             put_shifted(i, j, errors)
 
-    over_patches(second)
+    inner_patches(second)
+    halo_arrived(1)
+    halo_arrived(2)
+    outer_patches(second)
     halo_start(3)
     out_one = pltpu.make_async_copy(q_o1, r1_out, out_sem.at[1])
     out_one.start()
@@ -469,15 +482,15 @@
     weight_gradient(1, p_ef, p_l)
     reduce_start(1)
     reduce_spread(0)
+
+    def third(i, pair):
+        spread = dot(band_tf[...], windows(p_ef, i, pair))
+        for r, j in enumerate(pair):
+            put(q_c2, i, j, (get(q_c2, i, j) + mask * join(spread, r)).astype(BF))
+
+    inner_patches(third)
     halo_arrived(3)
-
-    def third(i, q):
-        spread = dot(band_tf[...], windows(p_ef, i, q))
-        for r in range(2):
-            j = 2 * q + r
-            put(q_c2, i, j, (get(q_c2, i, j) + mask * join(spread, r)).astype(BF))
-
-    over_patches(third)
+    outer_patches(third)
     out_last = pltpu.make_async_copy(q_c2, g2_out, out_sem.at[3])
     out_last.start()
     reduce_middle(1)

time: 110 us -> 76.9 us (0.70)
  Pallas kernels: 109 us -> 75.8 us
    pallas_call x1, Pallas kernels: 97.6 us -> 64.8 us  [local(): pl.pallas_call(fused, out_shape=(turned, turned, turned, turned, sums, su...]
where the time goes in v2:
time: 76.9 us; the launch traced here: 76.6 us
  Pallas kernels  75.8 us (99%)
  between operations  0.82 us (1%)
    pallas_call x1, Pallas kernels, local(): pl.pallas_call(fused, out_shape=(turned, turned, turned, turned, sums, su...  64.8 us
    pallas_call x1, Pallas kernels, local(): pl.pallas_call(back, grid=(8,), out_shape=(volume, volume, volume, volume...  11 us

profile of v2, /device:TPU:1, one launch (start us, length us, event | category | flops | bytes accessed | tf_op | source)
XLA Modules:
  0.0 76.6 jit_solution(4595925624387246847)
XLA Ops:
  0.6 64.8 %fused.1 = (bf16[16,16,32,128]{3,2,1,0:T(8,128)(2,1)}, bf16[16,16,32,128]{3,2,1,0:T(8,128)(2,1)}, bf16[16,16,32,128]{3,2,1,0:T(8,128)(2,1)}, bf16[16,16,32,128]{...) custom-call(bf16[32,16,16,128]{3,2,1,0:T(8,128)(2,1)} %o1.1, bf16[32,16,16,128]{3,2,1,0:T(8,128)(2,1)} %o2.1, ...), custom_call_target="tpu_custom_call" | custom-call | tf_op jit(solution)/shard_map/fused/pallas_call | solution.py:542
  65.5 11.0 %natural.1 = (bf16[32,16,16,128]{3,2,1,0:T(8,128)(2,1)}, bf16[32,16,16,128]{3,2,1,0:T(8,128)(2,1)}, bf16[32,16,16,128]{3,2,1,0:T(8,128)(2,1)}, bf16[32,16,16,128...) custom-call(bf16[16,16,32,128]{3,2,1,0:T(8,128)(2,1)} %get-tuple-element.12.refs_0_, ...), custom_call_target="tpu_custom_call" | custom-call | tf_op jit(solution)/shard_map/natural/pallas_call | solution.py:590

commit v3 on v2

--- a/solution.py
+++ b/solution.py
@@ -17,7 +17,8 @@
 ND = 16
 NG = 8
 CHUNKS = 12
-DIRS = tuple((dz, dy) for dz in (-1, 0, 1) for dy in (-1, 0, 1) if (dz, dy) != (0, 0))
+DIRS = ((0, -1), (0, 1), (-1, 0), (1, 0), (-1, -1), (-1, 1), (1, -1), (1, 1))
+SIDES, ENDS, CORNERS = (0, 1), (2, 3), (4, 5, 6, 7)
 
 
 def dot(a, b):
@@ -78,13 +79,12 @@
 
 def fused(
     o1, o2, c1, c2, w1_ref, w2_ref, bricks_ref,
-    r1_out, r2_out, g1_out, g2_out, t1_out, t2_out,
+    q_o1, q_o2, q_c1, q_c2, t1_out, t2_out,
     n_o1, n_o2, n_c1, n_c2,
-    q_o1, q_o2, q_c1, q_c2,
-    p_u, p_l, p_eg, p_ef,
+    p_u, p_pair, p_ef,
     shifted, perm, band_f, band_g, band_tf, band_tg, acc,
     part, rs_in, ar_in, tot,
-    in_sem, out_sem, hs, hr, rs_s, rs_r, ar_s, ar_r, ag_s, ag_r,
+    in_sem, hs, hr, rs_s, rs_r, ar_s, ar_r, ag_s, ag_r,
 ):
     depth = lax.axis_index("depth")
     group = lax.axis_index("group")
@@ -108,8 +108,7 @@
         pltpu.make_async_copy(src, dst, in_sem.at[n])
         for n, (src, dst) in enumerate(((o1, n_o1), (c2, n_c2), (o2, n_o2), (c1, n_c1)))
     ]
-    for load in loads:
-        load.start()
+    loads[0].start()
 
     barrier = pltpu.get_barrier_semaphore()
 
@@ -125,8 +124,8 @@
         )
         return 0
 
-    lax.fori_loop(1, ND, greet_depth, 0)
-    lax.fori_loop(1, NG, greet_group, 0)
+    lax.fori_loop(1, ND, greet_depth, 0, unroll=ND - 1)
+    lax.fori_loop(1, NG, greet_group, 0, unroll=NG - 1)
     for dz, dy in DIRS:
         if dz != 0 and dy != 0:
 
@@ -140,7 +139,8 @@
     for slot in range(8):
         mask = jnp.where(place == bricks_ref[0, group, slot], 1.0, mask)
 
-    volumes = (p_u, p_l, p_eg, p_ef)
+    p_l, p_eg = p_pair.at[0], p_pair.at[1]
+    volumes = (p_u, p_pair, p_ef)
 
     def zero_plane(ref, z):
         def body(y, _):
@@ -160,14 +160,14 @@
 
         @pl.when(d)
         def _():
-            for ref in volumes:
+            for ref in (p_u, p_l, p_eg, p_ef):
                 zero_plane(ref, at)
 
     for d, at in ((group == 0, 0), (group == NG - 1, B + 1)):
 
         @pl.when(d)
         def _():
-            for ref in volumes:
+            for ref in (p_u, p_l, p_eg, p_ef):
                 zero_row(ref, at)
 
     def relayout(src, dst, masked=None):
@@ -198,9 +198,10 @@
     def halo(number, k):
         dz, dy = DIRS[k]
         ref = volumes[number]
+        both = (pl.ds(0, 2),) if number == 1 else ()
         return pltpu.make_async_remote_copy(
-            src_ref=ref.at[side(dz, True), side(dy, True)],
-            dst_ref=ref.at[side(dz, False), side(dy, False)],
+            src_ref=ref.at[*both, side(dz, True), side(dy, True)],
+            dst_ref=ref.at[*both, side(dz, False), side(dy, False)],
             send_sem=hs.at[number, k],
             recv_sem=hr.at[number, k],
             device_id=clamp(dz, dy),
@@ -214,8 +215,9 @@
             def _():
                 halo(number, k).start()
 
-    def halo_arrived(number):
-        for k, (dz, dy) in enumerate(DIRS):
+    def halo_arrived(number, which):
+        for k in which:
+            dz, dy = DIRS[k]
 
             @pl.when(exists(-dz, -dy))
             def _():
@@ -259,18 +261,23 @@
 
         lax.fori_loop(1, 7, step, 0, unroll=6)
 
-    def outer_patches(body):
-        def sides(i, _):
+    def outer_patches(body, number):
+        def end(n, _):
+            j = 2 * lax.rem(n, 3) + 1
+            body(7 * lax.div(n, 3), (j, j + 1))
+            return 0
+
+        def edge(i, _):
             body(i, (0, 7))
             return 0
 
-        def ends(n, _):
-            j = 2 * lax.rem(n, 4)
-            body(7 * lax.div(n, 4), (j, j + 1))
-            return 0
-
-        lax.fori_loop(1, 7, sides, 0, unroll=6)
-        lax.fori_loop(0, 8, ends, 0, unroll=8)
+        halo_arrived(number, ENDS)
+        lax.fori_loop(0, 6, end, 0, unroll=6)
+        halo_arrived(number, SIDES)
+        lax.fori_loop(1, 7, edge, 0, unroll=6)
+        halo_arrived(number, CORNERS)
+        body(0, (0, 7))
+        body(7, (0, 7))
 
     def sigmoid(v):
         return 0.5 + 0.5 * jnp.tanh(0.5 * v)
@@ -302,74 +309,43 @@
                     total = rows if total is None else total + rows
             part[w, 4 * c : 4 * c + 4] = total[:, :384].reshape(4, 8, 384)
 
+    own = lax.rem(depth, CHUNKS)
+    owner = depth < CHUNKS
+
     def rs_copy(w, k):
         peer = lax.rem(depth + k, ND)
         return pltpu.make_async_remote_copy(
             src_ref=part.at[w, lax.rem(peer, CHUNKS)],
             dst_ref=rs_in.at[w, depth],
-            send_sem=rs_s.at[w, k],
-            recv_sem=rs_r.at[w, depth],
+            send_sem=rs_s.at[w],
+            recv_sem=rs_r.at[w],
             device_id=(peer, group),
             device_id_type=MESH,
         )
 
-    def rs_arrival(w, k):
-        peer = lax.rem(depth + k, ND)
-        return pltpu.make_async_remote_copy(
-            src_ref=part.at[w, 0],
-            dst_ref=rs_in.at[w, peer],
-            send_sem=rs_s.at[w, k],
-            recv_sem=rs_r.at[w, peer],
-            device_id=(peer, group),
-            device_id_type=MESH,
-        )
-
     def ar_copy(w, k):
-        peer = lax.rem(group + k, NG)
         return pltpu.make_async_remote_copy(
             src_ref=ar_in.at[w, group],
             dst_ref=ar_in.at[w, group],
-            send_sem=ar_s.at[w, k],
-            recv_sem=ar_r.at[w, group],
-            device_id=(depth, peer),
+            send_sem=ar_s.at[w],
+            recv_sem=ar_r.at[w],
+            device_id=(depth, lax.rem(group + k, NG)),
             device_id_type=MESH,
         )
 
-    def ar_arrival(w, k):
-        peer = lax.rem(group + k, NG)
+    def ag_copy(w, k):
         return pltpu.make_async_remote_copy(
-            src_ref=ar_in.at[w, group],
-            dst_ref=ar_in.at[w, peer],
-            send_sem=ar_s.at[w, k],
-            recv_sem=ar_r.at[w, peer],
-            device_id=(depth, peer),
+            src_ref=tot.at[w, own],
+            dst_ref=tot.at[w, own],
+            send_sem=ag_s.at[w],
+            recv_sem=ag_r.at[w],
+            device_id=(lax.rem(depth + k, ND), group),
             device_id_type=MESH,
         )
 
-    def ag_copy(w, k):
-        peer = lax.rem(depth + k, ND)
-        return pltpu.make_async_remote_copy(
-            src_ref=tot.at[w, lax.rem(depth, CHUNKS)],
-            dst_ref=tot.at[w, lax.rem(depth, CHUNKS)],
-            send_sem=ag_s.at[w, k],
-            recv_sem=ag_r.at[w, lax.rem(depth, CHUNKS)],
-            device_id=(peer, group),
-            device_id_type=MESH,
-        )
-
-    def ag_arrival(w, k):
-        peer = lax.rem(depth + k, ND)
-        at = lax.rem(peer, CHUNKS)
-        return pltpu.make_async_remote_copy(
-            src_ref=tot.at[w, at],
-            dst_ref=tot.at[w, at],
-            send_sem=ag_s.at[w, k],
-            recv_sem=ag_r.at[w, at],
-            device_id=(peer, group),
-            device_id_type=MESH,
-        )
-
-    owner = depth < CHUNKS
+    def await_chunks(sem, w, count):
+        ref = rs_in.at[w, pl.ds(0, count)]
+        pltpu.make_async_copy(ref, ref, sem.at[w]).wait()
 
     def each_peer(size, act, only_owners=False):
         def body(k, _):
@@ -382,7 +358,7 @@
                 act(k)
             return 0
 
-        lax.fori_loop(1, size, body, 0)
+        lax.fori_loop(1, size, body, 0, unroll=size - 1)
 
     def reduce_start(w):
         each_peer(ND, lambda k: rs_copy(w, k).start(), True)
@@ -390,29 +366,35 @@
     def reduce_middle(w):
         @pl.when(owner)
         def _():
-            rs_in[w, depth] = part[w, lax.rem(depth, CHUNKS)]
-            each_peer(ND, lambda k: rs_arrival(w, k).wait_recv())
+            rs_in[w, depth] = part[w, own]
+            await_chunks(rs_r, w, ND - 1)
             ar_in[w, group] = jnp.sum(rs_in[w], axis=0)
             each_peer(NG, lambda k: ar_copy(w, k).start())
 
     def reduce_spread(w):
         @pl.when(owner)
         def _():
-            each_peer(NG, lambda k: ar_arrival(w, k).wait_recv())
-            tot[w, lax.rem(depth, CHUNKS)] = jnp.sum(ar_in[w], axis=0)
+            await_chunks(ar_r, w, NG - 1)
+            tot[w, own] = jnp.sum(ar_in[w], axis=0)
             each_peer(ND, lambda k: ag_copy(w, k).start())
 
     def reduce_end(w):
-        each_peer(ND, lambda k: ag_arrival(w, k).wait_recv(), True)
-        each_peer(ND, lambda k: rs_copy(w, k).wait_send(), True)
-
         @pl.when(owner)
         def _():
-            each_peer(NG, lambda k: ar_copy(w, k).wait_send())
-            each_peer(ND, lambda k: ag_copy(w, k).wait_send())
+            await_chunks(ag_r, w, CHUNKS - 1)
+            await_chunks(rs_s, w, CHUNKS - 1)
+            await_chunks(ar_s, w, NG - 1)
+            await_chunks(ag_s, w, ND - 1)
+
+        @pl.when(jnp.logical_not(owner))
+        def _():
+            await_chunks(ag_r, w, CHUNKS)
+            await_chunks(rs_s, w, CHUNKS)
 
     build_band(w2_ref, band_g)
     loads[0].wait()
+    for load in loads[1:]:
+        load.start()
     relayout(n_o1, q_o1, p_u)
     near = jnp.minimum(depth, 1) + jnp.minimum(ND - 1 - depth, 1)
     aside = jnp.minimum(group, 1) + jnp.minimum(NG - 1 - group, 1)
@@ -444,12 +426,8 @@
             put_shifted(i, j, errors)
 
     inner_patches(first)
-    halo_arrived(0)
-    outer_patches(first)
+    outer_patches(first, 0)
     halo_start(1)
-    halo_start(2)
-    out_two = pltpu.make_async_copy(q_o2, r2_out, out_sem.at[0])
-    out_two.start()
     weight_gradient(0, p_eg, p_u)
     reduce_start(0)
 
@@ -470,15 +448,9 @@
             put_shifted(i, j, errors)
 
     inner_patches(second)
-    halo_arrived(1)
-    halo_arrived(2)
-    outer_patches(second)
-    halo_start(3)
-    out_one = pltpu.make_async_copy(q_o1, r1_out, out_sem.at[1])
-    out_one.start()
-    out_grad = pltpu.make_async_copy(q_c1, g1_out, out_sem.at[2])
-    out_grad.start()
     reduce_middle(0)
+    outer_patches(second, 1)
+    halo_start(2)
     weight_gradient(1, p_ef, p_l)
     reduce_start(1)
     reduce_spread(0)
@@ -489,53 +461,64 @@
             put(q_c2, i, j, (get(q_c2, i, j) + mask * join(spread, r)).astype(BF))
 
     inner_patches(third)
-    halo_arrived(3)
-    outer_patches(third)
-    out_last = pltpu.make_async_copy(q_c2, g2_out, out_sem.at[3])
-    out_last.start()
     reduce_middle(1)
+    outer_patches(third, 2)
     reduce_spread(1)
     reduce_end(0)
     reduce_end(1)
-    for number in range(4):
+    for number in range(3):
         halo_sent(number)
     t2_out[...] = tot[0]
     t1_out[...] = tot[1]
-    for copy in (out_two, out_one, out_grad, out_last):
+
+
+def natural(
+    scale, r1, r2, g1, g2, t1, t2,
+    r1_out, r2_out, g1_out, g2_out, w1_out, w2_out,
+    n1, n2, n3, n4, perm, sems,
+):
+    perm[...] = permutation()
+    copies = []
+    for number, (src, wide, out) in enumerate(
+        ((r1, n1, r1_out), (r2, n2, r2_out), (g1, n3, g1_out), (g2, n4, g2_out))
+    ):
+        for h in range(2):
+
+            def body(k, _):
+                pair = jnp.concatenate(
+                    [src[2 * k + zz, :, 16 * h : 16 * h + 16, :].reshape(256, NX) for zz in range(2)],
+                    axis=1,
+                )
+                turned = dot(perm[...], pair)
+                for zz in range(2):
+                    half = turned[:, NX * zz : NX * (zz + 1)]
+                    wide[16 * h : 16 * h + 16, 2 * k + zz] = half.astype(BF).reshape(16, 16, NX)
+                return 0
+
+            lax.fori_loop(0, 8, body, 0, unroll=8)
+            copy = pltpu.make_async_copy(
+                wide.at[pl.ds(16 * h, 16)], out.at[pl.ds(16 * h, 16)], sems.at[number, h]
+            )
+            copy.start()
+            copies.append(copy)
+    for src, dst in ((t1, w1_out), (t2, w2_out)):
+        for c in range(3):
+            rows = src[4 * c : 4 * c + 4].reshape(CH, 384) * scale
+            for a in range(3):
+                for b in range(3):
+                    at = (a * 4 + b) * CH
+                    dst[9 * a + 3 * b + c] = rows[:, at : at + CH]
+    for copy in copies:
         copy.wait()
 
 
-def natural(scale, r1, r2, g1, g2, t1, t2, r1_out, r2_out, g1_out, g2_out, w1_out, w2_out):
-    perm = permutation()
-    for src, dst in ((r1, r1_out), (r2, r2_out), (g1, g1_out), (g2, g2_out)):
-        for h in range(2):
-            pair = jnp.concatenate(
-                [src[zz, :, 16 * h : 16 * h + 16, :].reshape(256, NX) for zz in range(2)], axis=1
-            )
-            turned = dot(perm, pair)
-            for zz in range(2):
-                half = turned[:, NX * zz : NX * (zz + 1)]
-                dst[16 * h : 16 * h + 16, zz] = half.astype(BF).reshape(16, 16, NX)
-
-    @pl.when(pl.program_id(0) == 0)
-    def _():
-        for src, dst in ((t1, w1_out), (t2, w2_out)):
-            for c in range(3):
-                rows = src[4 * c : 4 * c + 4].reshape(CH, 384) * scale
-                for a in range(3):
-                    for b in range(3):
-                        at = (a * 4 + b) * CH
-                        dst[9 * a + 3 * b + c] = rows[:, at : at + CH]
-
-
 def local(output_one, output_two, cotangent_one, cotangent_two, first_weight, second_weight, bricks):
-    turned = jax.ShapeDtypeStruct((B, B, CH, NX), BF)
-    sums = jax.ShapeDtypeStruct((CHUNKS, 8, 384), F32)
+    turned = pltpu.VMEM((B, B, CH, NX), BF)
+    sums = pltpu.VMEM((CHUNKS, 8, 384), F32)
     hbm = pl.BlockSpec(memory_space=pl.ANY)
     vmem = pl.BlockSpec(memory_space=pltpu.VMEM)
     smem = pl.BlockSpec(memory_space=pltpu.SMEM)
     plain = pltpu.VMEM((CH, B, B, NX), BF)
-    flipped = pltpu.VMEM((B, B, CH, NX), BF)
     padded = pltpu.VMEM((B + 2, B + 2, CH, NX), BF)
     band = pltpu.VMEM((384, 512), BF)
     dma = pltpu.SemaphoreType.DMA
@@ -543,10 +526,9 @@
         fused,
         out_shape=(turned, turned, turned, turned, sums, sums),
         in_specs=[hbm, hbm, hbm, hbm, vmem, vmem, smem],
-        out_specs=(hbm, hbm, hbm, hbm, vmem, vmem),
+        out_specs=(vmem,) * 6,
         scratch_shapes=[plain] * 4
-        + [flipped] * 4
-        + [padded] * 4
+        + [padded, pltpu.VMEM((2, B + 2, B + 2, CH, NX), BF), padded]
         + [
             pltpu.VMEM((2, B, B, CH, NX), BF),
             pltpu.VMEM((256, 256), BF),
@@ -560,27 +542,22 @@
             pltpu.VMEM((2, NG, 8, 384), F32),
             pltpu.VMEM((2, CHUNKS, 8, 384), F32),
             dma((4,)),
-            dma((4,)),
-            dma((4, 8)),
-            dma((4, 8)),
-            dma((2, ND)),
-            dma((2, ND)),
-            dma((2, NG)),
-            dma((2, NG)),
-            dma((2, ND)),
-            dma((2, CHUNKS)),
+            dma((3, 8)),
+            dma((3, 8)),
+            dma((2,)),
+            dma((2,)),
+            dma((2,)),
+            dma((2,)),
+            dma((2,)),
+            dma((2,)),
         ],
         compiler_params=pltpu.CompilerParams(
-            collective_id=0, has_side_effects=True, vmem_limit_bytes=56 * 1024 * 1024
+            collective_id=0, has_side_effects=True, vmem_limit_bytes=51 * 1024 * 1024
         ),
         name="fused",
     )(output_one, output_two, cotangent_one, cotangent_two, first_weight, second_weight, bricks)
 
     scale = 1.0 / math.sqrt(float(B * ND * B * NG * NX))
-    block = pl.BlockSpec((2, B, CH, NX), lambda k: (k, 0, 0, 0))
-    result = pl.BlockSpec((CH, 2, B, NX), lambda k: (0, k, 0, 0))
-    whole = pl.BlockSpec((CHUNKS, 8, 384), lambda k: (0, 0, 0))
-    taps = pl.BlockSpec((27, CH, CH), lambda k: (0, 0, 0))
     volume = jax.ShapeDtypeStruct((CH, B, B, NX), BF)
     weight = jax.ShapeDtypeStruct((27, CH, CH), F32)
 
@@ -589,10 +566,11 @@
 
     return pl.pallas_call(
         back,
-        grid=(8,),
         out_shape=(volume, volume, volume, volume, weight, weight),
-        in_specs=[block, block, block, block, whole, whole],
-        out_specs=(result, result, result, result, taps, taps),
+        in_specs=[vmem] * 6,
+        out_specs=(hbm, hbm, hbm, hbm, vmem, vmem),
+        scratch_shapes=[plain] * 4 + [pltpu.VMEM((256, 256), BF), dma((4, 2))],
+        compiler_params=pltpu.CompilerParams(vmem_limit_bytes=20 * 1024 * 1024),
         name="natural",
     )(r1, r2, g1, g2, t1, t2)
 

time: 76.9 us -> 64.3 us (0.84)
  Pallas kernels: 75.8 us -> 63.3 us
    pallas_call x1, Pallas kernels: 11 us -> 4.72 us  [local(): pl.pallas_call(back, out_shape=(volume, volume, volume, volume, weight, w...]
    pallas_call x1, Pallas kernels: 64.8 us -> 58.6 us  [local(): pl.pallas_call(fused, out_shape=(turned, turned, turned, turned, sums, su...]
where the time goes in v3:
time: 64.3 us; the launch traced here: 64.1 us
  Pallas kernels  63.3 us (98%)
  between operations  0.82 us (1%)
    pallas_call x1, Pallas kernels, local(): pl.pallas_call(fused, out_shape=(turned, turned, turned, turned, sums, su...  58.6 us
    pallas_call x1, Pallas kernels, local(): pl.pallas_call(back, out_shape=(volume, volume, volume, volume, weight, w...  4.72 us

profile of v3, /device:TPU:1, one launch (start us, length us, event | category | flops | bytes accessed | tf_op | source)
XLA Modules:
  0.0 64.1 jit_solution(12645875054222899173)
XLA Ops:
  0.6 58.6 %fused.1 = (bf16[16,16,32,128]{3,2,1,0:T(8,128)(2,1)S(1)}, bf16[16,16,32,128]{3,2,1,0:T(8,128)(2,1)S(1)}, bf16[16,16,32,128]{3,2,1,0:T(8,128)(2,1)S(1)}, bf16[16...) custom-call(bf16[32,16,16,128]{3,2,1,0:T(8,128)(2,1)} %o1.1, ...), custom_call_target="tpu_custom_call" | custom-call | tf_op jit(solution)/shard_map/fused/pallas_call | solution.py:525
  59.2 4.7 %natural.1 = (bf16[32,16,16,128]{3,2,1,0:T(8,128)(2,1)}, bf16[32,16,16,128]{3,2,1,0:T(8,128)(2,1)}, bf16[32,16,16,128]{3,2,1,0:T(8,128)(2,1)}, bf16[32,16,16,128...) custom-call(bf16[16,16,32,128]{3,2,1,0:T(8,128)(2,1)S(1)} %get-tuple-element.12.refs_0_, ...), custom_call_target="tpu_custom_call" | custom-call | tf_op jit(solution)/shard_map/natural/pallas_call | solution.py:567

commit v4 on v3

--- a/solution.py
+++ b/solution.py
@@ -448,12 +448,11 @@
             put_shifted(i, j, errors)
 
     inner_patches(second)
-    reduce_middle(0)
     outer_patches(second, 1)
     halo_start(2)
+    reduce_middle(0)
     weight_gradient(1, p_ef, p_l)
     reduce_start(1)
-    reduce_spread(0)
 
     def third(i, pair):
         spread = dot(band_tf[...], windows(p_ef, i, pair))
@@ -461,6 +460,7 @@
             put(q_c2, i, j, (get(q_c2, i, j) + mask * join(spread, r)).astype(BF))
 
     inner_patches(third)
+    reduce_spread(0)
     reduce_middle(1)
     outer_patches(third, 2)
     reduce_spread(1)

time: 64.3 us -> 62.7 us (0.975)
  Pallas kernels: 63.3 us -> 61.7 us
    pallas_call x1, Pallas kernels: 58.6 us -> 57 us  [local(): pl.pallas_call(fused, out_shape=(turned, turned, turned, turned, sums, su...]
where the time goes in v4:
time: 62.7 us; the launch traced here: 62.5 us
  Pallas kernels  61.7 us (98%)
  between operations  0.82 us (1%)
    pallas_call x1, Pallas kernels, local(): pl.pallas_call(fused, out_shape=(turned, turned, turned, turned, sums, su...  57 us
    pallas_call x1, Pallas kernels, local(): pl.pallas_call(back, out_shape=(volume, volume, volume, volume, weight, w...  4.72 us

profile of v4, /device:TPU:1, one launch (start us, length us, event | category | flops | bytes accessed | tf_op | source)
XLA Modules:
  0.0 62.5 jit_solution(1251899971733339922)
XLA Ops:
  0.6 57.0 %fused.1 = (bf16[16,16,32,128]{3,2,1,0:T(8,128)(2,1)S(1)}, bf16[16,16,32,128]{3,2,1,0:T(8,128)(2,1)S(1)}, bf16[16,16,32,128]{3,2,1,0:T(8,128)(2,1)S(1)}, bf16[16...) custom-call(bf16[32,16,16,128]{3,2,1,0:T(8,128)(2,1)} %o1.1, ...), custom_call_target="tpu_custom_call" | custom-call | tf_op jit(solution)/shard_map/fused/pallas_call | solution.py:525
  57.6 4.7 %natural.1 = (bf16[32,16,16,128]{3,2,1,0:T(8,128)(2,1)}, bf16[32,16,16,128]{3,2,1,0:T(8,128)(2,1)}, bf16[32,16,16,128]{3,2,1,0:T(8,128)(2,1)}, bf16[32,16,16,128...) custom-call(bf16[16,16,32,128]{3,2,1,0:T(8,128)(2,1)S(1)} %get-tuple-element.12.refs_0_, ...), custom_call_target="tpu_custom_call" | custom-call | tf_op jit(solution)/shard_map/natural/pallas_call | solution.py:567
